TPU v7x, 128 devices: a whole 4x4x4 slice. The times are simulated.
128 devices in a mesh: tile: 32 (over z, y, core), slab: 4 (over x).
Axes of the slice: x: 4, y: 4, z: 4, core: 2. Of those that a mesh axis runs over, the one named last changes fastest.
Arguments:
- snapshots: float32 [64, 245760], P('tile', 'slab'), as said below
- old_basis: float32 [245760, 512], P(('slab', 'tile'))
- sing_values: float32 [512], replicated, may hold values from 2 to 8
Outputs:
- new_basis: bfloat16 [245760, 512], P(('slab', 'tile'))
Inputs may be any that keep to these rules, and one draw needn't show every extreme that they name: Each snapshot is a combination of the resident modes plus a residual part whose size differs strongly between snapshots and grows along the cells.
All inputs are finite; a program needn't handle non-finite values.
Results may differ from a plain program's by a relative error of at most 0.001.
Values sent between devices are 32-bit elements; how exact they have to be, the bound alone decides.
A program may use at most 64 MiB of HBM per device.

v0:
```python
import jax
import jax.numpy as jnp
from jax import lax
from jax.sharding import Mesh
from jax.sharding import PartitionSpec as P

TILE = ("tile_0", "tile_1", "tile_2")
SLAB_TILE = ("slab", "tile_0", "tile_1", "tile_2")


HIGH = lax.Precision.HIGHEST


def rows_for(lines, devices):
    spare = -lines.shape[0] % devices
    if not spare:
        return lines
    return jnp.concatenate([lines, jnp.zeros((spare, *lines.shape[1:]), lines.dtype)])


def copy_for_each(shard, axis):
    copies = jnp.broadcast_to(shard, (lax.axis_size(axis), *shard.shape))
    return lax.all_to_all(copies, axis, split_axis=0, concat_axis=0, tiled=True)


def joined_along(parts, dim):
    parts = jnp.moveaxis(parts, 0, dim)
    shape = parts.shape
    return parts.reshape(*shape[:dim], shape[dim] * shape[dim + 1], *shape[dim + 2 :])


def gathered_by_axis(shard, axes, dim):
    far, near = axes
    leading = copy_for_each(shard, far)
    parts = jnp.swapaxes(copy_for_each(leading, near), 0, 1)
    return joined_along(parts.reshape(-1, *shard.shape), dim)


def cut_along(shard, dim, devices):
    shape = shard.shape
    parts = shard.reshape(*shape[:dim], devices, shape[dim] // devices, *shape[dim + 1 :])
    return jnp.moveaxis(parts, dim, 0)


def sum_at_owner(shard, axis, dim):
    devices = lax.axis_size(axis)
    parts = lax.all_to_all(cut_along(shard, dim, devices), axis, 0, 0, tiled=True)
    return jnp.sum(parts, axis=0)


def sum_in_two_steps(shard, axes, dim):
    far, near = axes
    own = sum_at_owner(cut_along(shard, dim, lax.axis_size(far)), near, dim + 1)
    return jnp.sum(lax.all_to_all(own, far, 0, 0, tiled=True), axis=0)


def sum_by_parts(shard, axes):
    padded = rows_for(shard, lax.axis_size(axes[0]) * lax.axis_size(axes[1]))
    whole = gathered_by_axis(sum_in_two_steps(padded, axes, 0), axes, 0)
    return lax.slice_in_dim(whole, 0, len(shard)).reshape(shard.shape)


def together(arrays, axis):
    flat, at, outs = (jnp.concatenate([a.reshape(-1) for a in arrays]), 0, [])
    subtotal = sum_by_parts(flat, axis)
    for a in arrays:
        outs.append(subtotal[at : at + a.size].reshape(a.shape))
        at += a.size
    return tuple(outs)


def tri_solve(lower, rows):
    return lax.linalg.triangular_solve(lower, rows, left_side=True, lower=True)


def rotation_of(coeffs, factor_mat, sing_values):
    upper_block = jnp.diag(sing_values * sing_values) + jnp.dot(
        coeffs.T, coeffs, precision=HIGH, preferred_element_type=jnp.float32
    )
    lower_block = jnp.dot(factor_mat.T, coeffs, precision=HIGH, preferred_element_type=jnp.float32)
    stacked = jnp.concatenate([upper_block, lower_block], axis=0)
    for repeat_index in range(2):
        gram_mat = jnp.dot(stacked.T, stacked, precision=HIGH, preferred_element_type=jnp.float32)
        lower = jnp.linalg.cholesky(gram_mat)
        stacked = tri_solve(lower, stacked.T).T
    return stacked


def inner_cells(left, right):
    return lax.dot_general(
        left, right, (((0,), (0,)), ((), ())), precision=HIGH, preferred_element_type=jnp.float32
    )


def local(snapshots, old_basis, sing_values):
    snap_rows = lax.all_to_all(snapshots, TILE, split_axis=1, concat_axis=0, tiled=True)
    cell_count = old_basis.shape[0] * lax.axis_size(TILE) * lax.axis_size("slab")
    weight_cell = 1.0 / cell_count
    local_coeffs = jnp.dot(snap_rows, old_basis, precision=HIGH, preferred_element_type=jnp.float32)
    local_snap = jnp.dot(snap_rows, snap_rows.T, precision=HIGH, preferred_element_type=jnp.float32)
    local_modes = inner_cells(old_basis, old_basis)
    summed_coeffs, summed_snap, summed_modes = together(
        (local_coeffs, local_snap, local_modes), (("tile_0", "tile_1"), ("tile_2", "slab"))
    )
    coeffs = summed_coeffs * weight_cell
    cross = jnp.dot(coeffs, coeffs.T, precision=HIGH, preferred_element_type=jnp.float32)
    shaped = jnp.dot(
        coeffs, summed_modes * weight_cell, precision=HIGH, preferred_element_type=jnp.float32
    )
    gram_res = (
        summed_snap * weight_cell
        - 2.0 * cross
        + jnp.dot(shaped, coeffs.T, precision=HIGH, preferred_element_type=jnp.float32)
    )
    resid = snap_rows - jnp.dot(
        coeffs, old_basis.T, precision=HIGH, preferred_element_type=jnp.float32
    )
    lower_one = jnp.linalg.cholesky(gram_res)
    ortho = tri_solve(lower_one, resid)
    rotation = rotation_of(coeffs, lower_one, sing_values)
    modes = old_basis.shape[1]
    result = jnp.dot(
        old_basis, rotation[:modes], precision=HIGH, preferred_element_type=jnp.float32
    )
    result = result + inner_cells(ortho, rotation[modes:])
    return result.astype(jnp.bfloat16)


def solution(mesh):
    torus = Mesh(
        mesh.devices.reshape(4, 4, 2, mesh.shape["slab"]), ("tile_0", "tile_1", "tile_2", "slab")
    )
    placed = (P(TILE, "slab"), P(SLAB_TILE, None), P())
    return jax.shard_map(
        local, mesh=torus, in_specs=placed, out_specs=P(SLAB_TILE, None), check_vma=False
    )
```

profile of v0, /device:TPU:1, one launch (start us, length us, event | category | flops | bytes accessed | tf_op | source)
XLA Modules:
  0.0 430.0 jit_solution(6186472650373264523)
XLA Ops:
  0.0 9.6 %all-to-all-start = ((f32[2,32,1920]{2,0,1:T(2,128)}), f32[2,32,1920]{2,0,1:T(2,128)S(1)}, u32[]{:S(2)}, u32[]{:S(2)}) async-start(f32[2,32,1920]{2,0,1:T(2,128)} %bitcast.144), calls=%async_computation | async-start | bytes 983040 | tf_op jit(solution)/shard_map/all_to_all | solution.py:96
  9.6 10.2 %convolution_bitcast_fusion = f32[64,4,8,128]{3,2,1,0:T(8,128)S(1)} fusion(f32[1920,512]{1,0:T(8,128)} %param.7), kind=kOutput, calls=%fused_computation.8 | convolution fusion | flops 6039797760 | bytes 4980736 | tf_op jit(solution)/shard_map/dot_general | solution.py:90
  20.0 0.8 all-to-all-done
  21.7 4.6 %convolution_bitcast_fusion.1 = f32[8,4,8,128]{3,2,1,0:T(8,128)S(1)} fusion(f32[64,1920]{1,0:T(8,128)S(1)} %all_to_all.35, f32[1920,512]{1,0:T(8,128)} %param.7), kind=kOutput, calls=%fused_computation.34 | convolution fusion | flops 754974720 | bytes 4554752 | tf_op jit(solution)/shard_map/dot_general | solution.py:99
  26.5 0.8 reshape_reshape.4
  27.3 1.3 copy.32
  28.6 4.7 %all-to-all-start.1 = ((f32[8,16,2336]{2,1,0:T(8,128)}), f32[8,16,2336]{2,1,0:T(8,128)S(1)}, u32[]{:S(2)}, u32[]{:S(2)}) async-start(f32[8,16,2336]{2,1,0:T(8,128)} %copy.32), calls=%async_computation.1 | async-start | bytes 2490368 | tf_op jit(solution)/shard_map/all_to_all | solution.py:47
  33.3 17.1 %all-to-all-done.1 = f32[8,16,2336]{2,1,0:T(8,128)S(1)} async-done(((f32[8,16,2336]{2,1,0:T(8,128)}), f32[8,16,2336]{2,1,0:T(8,128)S(1)}, u32[]{:S(2)}, u32[]{:S(2)}) %all-to-all-start.1) | async-done | bytes 1196064 | tf_op jit(solution)/shard_map/all_to_all | solution.py:47
  50.6 12.7 %all_to_all.48 = f32[16,1,2336]{2,1,0:T(1,128)S(1)} all-to-all(f32[16,1,2336]{2,1,0:T(1,128)S(1)} %all_to_all.37), channel_id=1, replica_groups=mesh['tile_0'=4,'tile_1'=4,'tile_2'=2,'slab'=4] {'tile_0','tile_1'}, dimensions={0} | all-to-all | bytes 299008 | tf_op jit(solution)/shard_map/all_to_all | solution.py:54
  63.4 10.0 %all_to_all.47 = f32[16,1,2336]{2,1,0:T(1,128)S(1)} all-to-all(f32[16,1,2336]{2,1,0:T(1,128)S(1)} %broadcast_in_dim.29), channel_id=1, replica_groups=mesh['tile_0'=4,'tile_1'=4,'tile_2'=2,'slab'=4] {'tile_0','tile_1'}, dimensions={0} | all-to-all | bytes 299008 | tf_op jit(solution)/shard_map/all_to_all | solution.py:23
  73.5 1.1 broadcast_in_dim.30
  74.6 7.0 %all-to-all-start.4 = ((f32[8,16,2336]{2,1,0:T(8,128)}), f32[8,16,2336]{2,1,0:T(8,128)S(1)}, u32[]{:S(2)}, u32[]{:S(2)}) async-start(f32[8,16,2336]{2,1,0:T(8,128)} %broadcast_in_dim.30), calls=%async_computation.4 | async-start | bytes 2490368 | tf_op jit(solution)/shard_map/all_to_all | solution.py:23
  81.6 16.6 %all-to-all-done.4 = f32[8,16,2336]{2,1,0:T(8,128)S(1)} async-done(((f32[8,16,2336]{2,1,0:T(8,128)}), f32[8,16,2336]{2,1,0:T(8,128)S(1)}, u32[]{:S(2)}, u32[]{:S(2)}) %all-to-all-start.4) | async-done | bytes 1196064 | tf_op jit(solution)/shard_map/all_to_all | solution.py:23
  98.7 0.9 slice.123
  99.6 6.7 %convolution_subtract_fusion = f32[64,1920]{1,0:T(8,128)} fusion(f32[64,1920]{1,0:T(8,128)S(1)} %all_to_all.35, f32[1920,512]{1,0:T(8,128)} %param.7, f32[584,512]{1,0:T(8,128)S(1)} %slice.123), kind=kOutput, calls=%fused_computation.6 | convolution fusion | flops 755130368 | bytes 5046272 | tf_op jit(solution)/shard_map/dot_general | solution.py:115
  106.3 0.8 fusion.12
  107.1 2.8 slice.125
  109.9 0.8 slice.177
  111.4 5.8 %cholesky.118 = f32[64,64]{1,0:T(8,128)S(1)} custom-call(f32[64,64]{1,0:T(8,128)S(1)} %fusion.83), custom_call_target="Cholesky" | custom-call | tf_op jit(solution)/shard_map/jit(cholesky)/cholesky | solution.py:118
  117.9 1.0 fusion.80
  118.9 0.7 select_bitcast_fusion.6
  119.5 1.0 convolution_add_fusion
  120.5 2.7 fusion.16
  123.4 5.7 %custom-call.29 = f32[1,64,64]{1,2,0:T(8,128)} custom-call(f32[1,64,64]{2,1,0:T(8,128)S(1)} %select_bitcast_fusion.6), custom_call_target="InvertDiagBlocksLowerTriangular" | custom-call | tf_op jit(solution)/shard_map/triangular_solve | solution.py:73
  129.6 1.0 copy-done.3
  130.6 11.7 %cholesky.324 = f32[128,128]{1,0:T(8,128)S(1)} custom-call(f32[128,128]{1,0:T(8,128)S(1)} %cholesky.464), custom_call_target="Cholesky" | custom-call | tf_op jit(solution)/shard_map/jit(cholesky)/cholesky | solution.py:84
  142.4 9.8 %custom-call.34 = f32[1,128,128]{1,2,0:T(8,128)S(1)} custom-call(f32[1,128,128]{2,1,0:T(8,128)S(1)} %get-tuple-element.62), custom_call_target="InvertDiagBlocksLowerTriangular" | custom-call | tf_op jit(solution)/shard_map/jit(cholesky)/cholesky | solution.py:84
  153.6 12.5 %cholesky.343 = f32[128,128]{1,0:T(8,128)S(1)} custom-call(f32[128,128]{1,0:T(8,128)} %cholesky.468), custom_call_target="Cholesky" | custom-call | tf_op jit(solution)/shard_map/jit(cholesky)/cholesky | solution.py:84
  166.2 0.6 fusion.77
  166.8 11.0 %custom-call.35 = f32[1,128,128]{1,2,0:T(8,128)S(1)} custom-call(f32[1,128,128]{2,1,0:T(8,128)} %get-tuple-element.59), custom_call_target="InvertDiagBlocksLowerTriangular" | custom-call | tf_op jit(solution)/shard_map/jit(cholesky)/cholesky | solution.py:84
  178.5 11.7 %cholesky.364 = f32[128,128]{1,0:T(8,128)S(1)} custom-call(f32[128,128]{1,0:T(8,128)S(1)} %cholesky.473), custom_call_target="Cholesky" | custom-call | tf_op jit(solution)/shard_map/jit(cholesky)/cholesky | solution.py:84
  190.2 0.7 compare_reduce_fusion.5
  191.0 9.8 %custom-call.36 = f32[1,128,128]{1,2,0:T(8,128)S(1)} custom-call(f32[1,128,128]{2,1,0:T(8,128)S(1)} %get-tuple-element.56), custom_call_target="InvertDiagBlocksLowerTriangular" | custom-call | tf_op jit(solution)/shard_map/jit(cholesky)/cholesky | solution.py:84
  201.4 11.9 %cholesky.381 = f32[128,128]{1,0:T(8,128)S(1)} custom-call(f32[128,128]{1,0:T(8,128)S(1)} %convolution_subtract_fusion.12), custom_call_target="Cholesky" | custom-call | tf_op jit(solution)/shard_map/jit(cholesky)/cholesky | solution.py:84
  213.9 0.7 compare_reduce_fusion.6
  217.3 8.5 %while.4 = (s32[]{:T(128)}, f32[512,512]{1,0:T(8,128)S(1)}, s32[4,2]{0,1:T(2,128)S(1)}, f32[4,128,128]{2,1,0:T(8,128)S(1)}, s32[]{:T(128)}) while((s32[]{:T(128)}, f32[512,512]{1,0:T(8,128)S(1)}, s32[4,2]{0,1:T(2,128)S(1)}, f32[4,128,128]{2,1,0:T(8,128)S(1)}, s32[]{:T(128)}) %tuple.51), condition=%wide.while_cond, body=%wide.while_body.sunk | while | flops 2 | bytes 131189 | solution.py:73
  218.0 1.4 bitcast_dynamic-update-slice_fusion.4
  220.1 1.4 bitcast_dynamic-update-slice_fusion.4
  222.2 1.4 bitcast_dynamic-update-slice_fusion.4
  224.3 1.4 bitcast_dynamic-update-slice_fusion.4
  225.8 39.3 %custom-call.37 = f32[4,128,128]{1,2,0:T(8,128)S(1)} custom-call(f32[4,128,128]{2,1,0:T(8,128)S(1)} %get-tuple-element.21), custom_call_target="InvertDiagBlocksLowerTriangular" | custom-call | tf_op jit(solution)/shard_map/triangular_solve/custom-call.8 | solution.py:73
  267.4 0.9 convolution_subtract_fusion.6
  268.7 2.7 fusion.1
  272.0 1.0 copy-done.1
  272.9 11.7 %cholesky.396 = f32[128,128]{1,0:T(8,128)S(1)} custom-call(f32[128,128]{1,0:T(8,128)S(1)} %cholesky.477), custom_call_target="Cholesky" | custom-call | tf_op jit(solution)/shard_map/jit(cholesky)/cholesky | solution.py:84
  284.7 0.7 compare_reduce_fusion.3
  285.4 10.0 %custom-call.38 = f32[1,128,128]{1,2,0:T(8,128)S(1)} custom-call(f32[1,128,128]{2,1,0:T(8,128)S(1)} %get-tuple-element.52), custom_call_target="InvertDiagBlocksLowerTriangular" | custom-call | tf_op jit(solution)/shard_map/jit(cholesky)/cholesky | solution.py:84
  296.2 11.7 %cholesky.415 = f32[128,128]{1,0:T(8,128)S(1)} custom-call(f32[128,128]{1,0:T(8,128)S(1)} %cholesky.481), custom_call_target="Cholesky" | custom-call | tf_op jit(solution)/shard_map/jit(cholesky)/cholesky | solution.py:84
  308.6 9.8 %custom-call.39 = f32[1,128,128]{1,2,0:T(8,128)S(1)} custom-call(f32[1,128,128]{2,1,0:T(8,128)S(1)} %get-tuple-element.49), custom_call_target="InvertDiagBlocksLowerTriangular" | custom-call | tf_op jit(solution)/shard_map/jit(cholesky)/cholesky | solution.py:84
  319.1 11.7 %cholesky.436 = f32[128,128]{1,0:T(8,128)S(1)} custom-call(f32[128,128]{1,0:T(8,128)S(1)} %cholesky.486), custom_call_target="Cholesky" | custom-call | tf_op jit(solution)/shard_map/jit(cholesky)/cholesky | solution.py:84
  331.5 10.2 %custom-call.40 = f32[1,128,128]{1,2,0:T(8,128)S(1)} custom-call(f32[1,128,128]{2,1,0:T(8,128)S(1)} %get-tuple-element.46), custom_call_target="InvertDiagBlocksLowerTriangular" | custom-call | tf_op jit(solution)/shard_map/jit(cholesky)/cholesky | solution.py:84
  342.2 11.7 %cholesky.453 = f32[128,128]{1,0:T(8,128)S(1)} custom-call(f32[128,128]{1,0:T(8,128)S(1)} %convolution_subtract_fusion.11), custom_call_target="Cholesky" | custom-call | tf_op jit(solution)/shard_map/jit(cholesky)/cholesky | solution.py:84
  354.0 0.7 compare_reduce_fusion
  357.3 8.5 %while.5 = (s32[]{:T(128)}, f32[512,512]{1,0:T(8,128)S(1)}, s32[4,2]{0,1:T(2,128)S(1)}, f32[4,128,128]{2,1,0:T(8,128)S(1)}, s32[]{:T(128)}) while((s32[]{:T(128)}, f32[512,512]{1,0:T(8,128)S(1)}, s32[4,2]{0,1:T(2,128)S(1)}, f32[4,128,128]{2,1,0:T(8,128)S(1)}, s32[]{:T(128)}) %tuple.57), condition=%wide.while_cond.clone, body=%wide.while_body.clone.sunk | while | flops 2 | bytes 131189 | solution.py:73
  358.0 1.4 bitcast_dynamic-update-slice_fusion.5
  360.1 1.4 bitcast_dynamic-update-slice_fusion.5
  362.3 1.4 bitcast_dynamic-update-slice_fusion.5
  364.4 1.4 bitcast_dynamic-update-slice_fusion.5
  365.8 39.5 %custom-call.41 = f32[4,128,128]{1,2,0:T(8,128)S(1)} custom-call(f32[4,128,128]{2,1,0:T(8,128)S(1)} %get-tuple-element.22), custom_call_target="InvertDiagBlocksLowerTriangular" | custom-call | tf_op jit(solution)/shard_map/triangular_solve/custom-call.8 | solution.py:73
  407.6 0.9 convolution_subtract_fusion.5
  409.0 0.7 copy-done
  409.7 13.7 %fusion.10 = f32[512,1920]{1,0:T(8,128)S(1)} fusion(f32[1920,512]{1,0:T(8,128)S(1)} %copy-done, f32[576,512]{1,0:T(8,128)S(1)} %maximum_bitcast_fusion), kind=kOutput, calls=%fused_computation.42 | convolution fusion | flops 6039797760 | bytes 8912896 | tf_op jit(solution)/shard_map/dot_general | solution.py:122
  424.1 3.4 fusion
  427.5 2.3 copy.42
  (108 shorter events, 23.1 us)
Async XLA Ops:
  0.0 20.8 %all-to-all-start = ((f32[2,32,1920]{2,0,1:T(2,128)}), f32[2,32,1920]{2,0,1:T(2,128)S(1)}, u32[]{:S(2)}, u32[]{:S(2)}) async-start(f32[2,32,1920]{2,0,1:T(2,128)} %bitcast.144), calls=%async_computation | async-start | bytes 983040 | tf_op jit(solution)/shard_map/all_to_all | solution.py:96
  28.6 21.8 %all-to-all-start.1 = ((f32[8,16,2336]{2,1,0:T(8,128)}), f32[8,16,2336]{2,1,0:T(8,128)S(1)}, u32[]{:S(2)}, u32[]{:S(2)}) async-start(f32[8,16,2336]{2,1,0:T(8,128)} %copy.32), calls=%async_computation.1 | async-start | bytes 2490368 | tf_op jit(solution)/shard_map/all_to_all | solution.py:47
  74.6 7.0 %copy-start.9 = (f32[512]{0:T(512)S(1)}, f32[512]{0:T(512)}, u32[]{:S(2)}) copy-start(f32[512]{0:T(512)} %param.8) | copy-start | bytes 6148
  74.6 23.6 %all-to-all-start.4 = ((f32[8,16,2336]{2,1,0:T(8,128)}), f32[8,16,2336]{2,1,0:T(8,128)S(1)}, u32[]{:S(2)}, u32[]{:S(2)}) async-start(f32[8,16,2336]{2,1,0:T(8,128)} %broadcast_in_dim.30), calls=%async_computation.4 | async-start | bytes 2490368 | tf_op jit(solution)/shard_map/all_to_all | solution.py:23
  129.6 1.0 copy-start.3
  130.6 21.7 %copy-start.4 = (f32[512,512]{1,0:T(8,128)S(1)}, f32[512,512]{1,0:T(8,128)}, u32[]{:S(2)}) copy-start(f32[512,512]{1,0:T(8,128)} %copy-done.3) | copy-start | bytes 3145732
  267.3 1.3 copy-start.5
  271.9 1.0 copy-start.1
  272.9 22.6 %copy-start.2 = (f32[512,512]{1,0:T(8,128)S(1)}, f32[512,512]{1,0:T(8,128)}, u32[]{:S(2)}) copy-start(f32[512,512]{1,0:T(8,128)} %copy-done.1) | copy-start | bytes 3145732
  365.8 40.7 %copy-start.6 = (f32[128,576]{0,1:T(8,128)S(1)}, f32[128,576]{0,1:T(8,128)}, u32[]{:S(2)}) copy-start(f32[128,576]{0,1:T(8,128)} %copy-done.5) | copy-start | bytes 884740
  407.6 2.1 copy-start
  409.7 13.8 %copy-start.7 = (f32[64,1920]{1,0:T(8,128)S(1)}, f32[64,1920]{1,0:T(8,128)}, u32[]{:S(2)}) copy-start(f32[64,1920]{1,0:T(8,128)} %convolution_subtract_fusion) | copy-start | bytes 1474564
  409.7 13.8 %copy-start.8 = (f32[1,64,64]{1,2,0:T(8,128)S(1)}, f32[1,64,64]{1,2,0:T(8,128)}, u32[]{:S(2)}) copy-start(f32[1,64,64]{1,2,0:T(8,128)} %custom-call.29) | copy-start | bytes 49156
where the time goes:
time: 438 us; the launch traced here: 430 us
  other arithmetic  254 us (58%)
  matrix products  59.3 us (14%)
  waiting for transfers between devices  34.5 us (8%)
  local copies, waits for them, and re-layouts  32.5 us (7%)
  blocking collectives  22.7 us (5%)
  starting transfers between devices  21.3 us (5%)
  between operations  6.04 us (1%)
    another operation x29, other arithmetic, rotation_of(): lower = jnp.linalg.cholesky(gram_mat)  161 us
    another operation x7, other arithmetic, tri_solve(): return lax.linalg.triangular_solve(lower, rows, left_side=True, lower=True)  85.4 us
    all_to_all x1, waiting for transfers between devices, sum_at_owner(): lax.all_to_all(cut_along(shard, dim, devices), axis, 0, 0, tiled=True)  17.1 us
    another operation x27, local copies, waits for them, and re-layouts, tri_solve(): return lax.linalg.triangular_solve(lower, rows, left_side=True, lower=True)  16.8 us
    all_to_all x1, waiting for transfers between devices, copy_for_each(): return lax.all_to_all(copies, axis, split_axis=0, concat_axis=0, tiled=True)  16.6 us
    dot_general x1, matrix products, local(): jnp.dot(old_basis, rotation[:modes], precision=HIGH, preferred_element_ty...  13.7 us
    dot_general x2, matrix products, inner_cells(): lax.dot_general(left, right, (((0,), (0,)), ((), ())), precision=HIGH, pr...  13.6 us
    all_to_all x1, blocking collectives, sum_in_two_steps(): return jnp.sum(lax.all_to_all(own, far, 0, 0, tiled=True), axis=0)  12.7 us
  transfers between devices with their start and end apart: 3, of which 3 were waited for; matrix products, arithmetic and copies ran while one was open for 2% of the time, Pallas kernels for 0%

commit v1 on v0

v1 whole, which is shorter than its diff:
```python
import functools

import jax
import jax.numpy as jnp
from jax import lax
from jax.experimental import pallas as pl
from jax.experimental.pallas import tpu as pltpu
from jax.sharding import PartitionSpec as P

F32, BF16 = jnp.float32, jnp.bfloat16
HIGH = lax.Precision.HIGHEST
BLK = 64


def dot6(a, b, ca=1, cb=0):
    return lax.dot_general(a, b, (((ca,), (cb,)), ((), ())), precision=HIGH, preferred_element_type=F32)


def split(a):
    hi = a.astype(BF16)
    return hi, (a - hi.astype(F32)).astype(BF16)


def dot1(a, b, ca=1, cb=0):
    return lax.dot_general(a, b, (((ca,), (cb,)), ((), ())), preferred_element_type=F32)


def dot3(a, b, ca=1, cb=0):
    (ah, al), (bh, bl) = split(a), split(b)
    return dot1(ah, bh, ca, cb) + (dot1(ah, bl, ca, cb) + dot1(al, bh, ca, cb))


def inverse_factors(mats):
    n = mats[0].shape[0]
    eye = (lax.broadcasted_iota(jnp.int32, (n, n), 0) == lax.broadcasted_iota(jnp.int32, (n, n), 1)).astype(F32)
    sub = lax.broadcasted_iota(jnp.int32, (8, 2 * n), 0)
    work = []
    for a in mats:
        both = jnp.concatenate([eye, a], axis=1)
        work.append([both[8 * r : 8 * r + 8] for r in range(n // 8)])
    scale = [[None] * (n // 8) for _ in mats]
    for j in range(n):
        r, s = divmod(j, 8)
        for m, rows in enumerate(work):
            row = jnp.broadcast_to(rows[r][s : s + 1, :], (8, 2 * n))
            pivot = jnp.broadcast_to(row[:, n + j : n + j + 1], (8, 2 * n))
            part = row * (1.0 / pivot)
            root = lax.rsqrt(pivot)
            scale[m][r] = root if s == 0 else jnp.where(sub == s, root, scale[m][r])
            for q in range(r, n // 8):
                col = jnp.broadcast_to(rows[q][:, n + j : n + j + 1], (8, 2 * n))
                if q == r:
                    col = jnp.where(sub > s, col, 0.0)
                rows[q] = rows[q] - col * part
    return [
        jnp.concatenate([rows[r] * scale[m][r] for r in range(n // 8)], axis=0)[:, :n]
        for m, rows in enumerate(work)
    ]


def weights_of(c, k_res, sing, second=True):
    snaps, modes = c.shape
    blocks = modes // BLK
    q = c / (sing * sing)
    lane = lax.broadcasted_iota(jnp.int32, (snaps, 128), 1)
    cp, cq, qq, cb, qb = [], [], [], [], []
    for k in range(blocks):
        at = (k // 2) * 128
        c2, q2 = c[:, at : at + 128], q[:, at : at + 128]
        mine = (lane // BLK) == (k % 2)
        cm, qm = jnp.where(mine, c2, 0.0), jnp.where(mine, q2, 0.0)
        cp.append(dot6(cm, c2, 1, 1))
        cq.append(dot6(cm, q2, 1, 1))
        qq.append(dot6(qm, q2, 1, 1))
        cb.append(c[:, k * BLK : (k + 1) * BLK])
        qb.append(q[:, k * BLK : (k + 1) * BLK])
    eye = (lax.broadcasted_iota(jnp.int32, (BLK, BLK), 0) == lax.broadcasted_iota(jnp.int32, (BLK, BLK), 1)).astype(F32)
    a, b, g = [None] * blocks, [None] * blocks, [None] * blocks
    run = k_res
    for k in reversed(range(blocks)):
        run = run + cp[k]
        a[k] = run
    runb, rung = eye, None
    for k in range(1, blocks):
        runb = runb + cq[k - 1]
        rung = qq[0] if k == 1 else rung + qq[k - 1]
        b[k], g[k] = runb, rung
    la = [None] + inverse_factors(a[1:])
    u = [None] + [dot6(la[k], b[k]) for k in range(1, blocks)]
    t = [None] + [dot6(la[k], cb[k]) for k in range(1, blocks)]
    lg = [None] + inverse_factors([g[k] + dot6(u[k], u[k], 0, 0) for k in range(1, blocks)])
    r = [None] + [dot6(lg[k], qb[k] + dot6(u[k], t[k], 0, 0)) for k in range(1, blocks)]
    s0 = eye + dot6(cb[0], qb[0], 0, 0) + dot6(qb[0], cb[0], 0, 0) + dot6(qb[0], dot6(a[0], qb[0]), 0, 0)
    ls = inverse_factors([s0] + [eye - dot6(t[k], t[k], 0, 0) + dot6(r[k], r[k], 0, 0) for k in range(1, blocks)])
    top, bot = [jnp.zeros((snaps, BLK), F32)], [jnp.zeros((snaps, BLK), F32)]
    for k in range(1, blocks):
        gk = dot6(lg[k], r[k], 0, 0)
        hk = dot6(la[k], dot6(u[k], gk) - t[k], 0, 0)
        top.append(dot6(hk, ls[k], 1, 1))
        bot.append(dot6(gk, ls[k], 1, 1))
    z = jnp.concatenate([jnp.concatenate(top, axis=1), jnp.concatenate(bot, axis=1)], axis=0)
    y = jnp.concatenate([c, q], axis=0)
    over = dot6(y, z, 0, 0)
    ri = lax.broadcasted_iota(jnp.int32, (modes, modes), 0) // BLK
    ci = lax.broadcasted_iota(jnp.int32, (modes, modes), 1) // BLK
    zero = jnp.zeros((BLK, BLK), F32)
    diag = jnp.concatenate(
        [jnp.concatenate([ls[k].T if j == k else zero for j in range(blocks)], axis=1) for k in range(blocks)], axis=0
    )
    w = diag - jnp.where(ri < ci, over, 0.0)
    v = dot6(q, w)
    if second:
        w, v = second_pass(c, k_res, w, v)
    return w, v


def second_pass(c, k_res, w, v):
    modes = c.shape[1]
    rot = w + dot3(c, v, 0, 0)
    gram = dot3(rot, rot, 0, 0) + dot3(v, dot3(k_res, v), 0, 0)
    ri = lax.broadcasted_iota(jnp.int32, (modes, modes), 0)
    ci = lax.broadcasted_iota(jnp.int32, (modes, modes), 1)
    half = jnp.where(ri < ci, gram, jnp.where(ri == ci, 0.5 * (gram - 1.0), 0.0)).astype(BF16)
    return w - dot1(w.astype(BF16), half), v - dot1(v.astype(BF16), half)


def update_kernel(c_ref, k_ref, s_ref, x_ref, u_ref, o_ref, wh_ref, wl_ref, vs_ref):
    @pl.when(pl.program_id(0) == 0)
    def _():
        w, v = weights_of(c_ref[...], k_ref[...], s_ref[...])
        wh, wl = split(w)
        wh_ref[...] = wh
        wl_ref[...] = wl
        vh, vl = split(v)
        vs_ref[...] = jnp.concatenate([vh, vl, vh], axis=0)

    uh, ul = split(u_ref[...])
    xh, xl = split(x_ref[...].T)
    xs = jnp.concatenate([xh, xh, xl], axis=1)
    wh = wh_ref[...]
    out = dot1(uh, wh) + dot1(uh, wl_ref[...]) + dot1(ul, wh) + dot1(xs, vs_ref[...])
    o_ref[...] = out.astype(BF16)


def update(c, k_res, sing, x, u, rows=384):
    cells, modes = u.shape
    snaps = x.shape[0]
    whole = lambda *shape: pl.BlockSpec(shape, lambda i: (0, 0))
    return pl.pallas_call(
        update_kernel,
        grid=(cells // rows,),
        out_shape=jax.ShapeDtypeStruct((cells, modes), BF16),
        in_specs=[
            whole(snaps, modes),
            whole(snaps, snaps),
            whole(1, modes),
            pl.BlockSpec((snaps, rows), lambda i: (0, i)),
            pl.BlockSpec((rows, modes), lambda i: (i, 0)),
        ],
        out_specs=pl.BlockSpec((rows, modes), lambda i: (i, 0)),
        scratch_shapes=[
            pltpu.VMEM((modes, modes), BF16),
            pltpu.VMEM((modes, modes), BF16),
            pltpu.VMEM((3 * snaps, modes), BF16),
        ],
        compiler_params=pltpu.CompilerParams(vmem_limit_bytes=48 * 2**20),
        cost_estimate=pl.CostEstimate(flops=2 * 3 * cells * modes * modes, bytes_accessed=6 * cells * modes, transcendentals=0),
    )(c, k_res, sing, x, u)


def local(snapshots, old_basis, sing_values):
    x = lax.all_to_all(snapshots, "tile", split_axis=1, concat_axis=0, tiled=True)
    cells = old_basis.shape[0] * lax.axis_size("tile") * lax.axis_size("slab")
    weight = 1.0 / cells
    c = jnp.dot(x, old_basis, precision=HIGH, preferred_element_type=F32)
    c = lax.psum(c, ("tile", "slab")) * weight
    resid = x - lax.dot_general(c, old_basis, (((1,), (1,)), ((), ())), precision=HIGH, preferred_element_type=F32)
    k_res = lax.dot_general(resid, resid, (((1,), (1,)), ((), ())), precision=HIGH, preferred_element_type=F32)
    k_res = lax.psum(k_res, ("tile", "slab")) * weight
    return update(c, k_res, sing_values[None], x, old_basis)


def solution(mesh):
    return jax.shard_map(
        local,
        mesh=mesh,
        in_specs=(P("tile", "slab"), P(("slab", "tile"), None), P()),
        out_specs=P(("slab", "tile"), None),
        check_vma=False,
    )
```

time: 438 us -> 298 us (0.68); the launches traced: 430 us -> 297 us
  other arithmetic: 254 us -> 0.02 us
  waiting for transfers between devices: 34.5 us -> 138 us
  blocking collectives: 22.7 us -> 84.2 us
  Pallas kernels: 0 us -> 47.6 us
  matrix products: 59.3 us -> 11.8 us
  local copies, waits for them, and re-layouts: 32.5 us -> 2.45 us
  starting transfers between devices: 21.3 us -> 0.01 us
  between operations: 6.04 us -> 13.4 us
    another operation x39 -> x0, other arithmetic: 253 us -> none  [the longest x29 161 us: rotation_of(): lower = jnp.linalg.cholesky(gram_mat)]
    psum x0 -> x1, waiting for transfers between devices: none -> 138 us  [local(): c = lax.psum(c, ('tile', 'slab')) * weight]
    psum x0 -> x1, blocking collectives: none -> 63.4 us  [local(): k_res = lax.psum(k_res, ('tile', 'slab')) * weight]
    pallas_call x0 -> x1, Pallas kernels: none -> 47.6 us  [update(): pl.pallas_call(update_kernel, grid=(cells // rows,), out_shape=jax.ShapeD...]
    dot_general x13 -> x3, matrix products: 47.9 us -> 11.8 us  [the longest x1 6 us: local(): lax.dot_general(c, old_basis, (((1,), (1,)), ((), ())), precision=HIGH, p...]
    all_to_all x3 -> x0, waiting for transfers between devices: 34.5 us -> none  [the longest x1 17.1 us: sum_at_owner(): lax.all_to_all(cut_along(shard, dim, devices), axis, 0, 0, tiled=True)]
    all_to_all x3 -> x0, starting transfers between devices: 21.3 us -> none  [the longest x1 9.6 us: local(): lax.all_to_all(snapshots, TILE, split_axis=1, concat_axis=0, tiled=True)]
    another operation x36 -> x0, local copies, waits for them, and re-layouts: 18.5 us -> none  [the longest x27 16.8 us: tri_solve(): return lax.linalg.triangular_solve(lower, rows, left_side=True, lower=True)]
  transfers between devices with their start and end apart: 3 -> 1, of which waited for: 3 -> 1; matrix products, arithmetic and copies ran while one was open for 2% -> 0% of each run, Pallas kernels for 0% -> 0%
where the time goes in v1:
time: 298 us; the launch traced here: 297 us
  waiting for transfers between devices  138 us (46%)
  blocking collectives  84.2 us (28%)
  Pallas kernels  47.6 us (16%)
  between operations  13.4 us (4%)
  matrix products  11.8 us (4%)
    psum x1, waiting for transfers between devices, local(): c = lax.psum(c, ('tile', 'slab')) * weight  138 us
    psum x1, blocking collectives, local(): k_res = lax.psum(k_res, ('tile', 'slab')) * weight  63.4 us
    pallas_call x1, Pallas kernels, update(): pl.pallas_call(update_kernel, grid=(cells // rows,), out_shape=jax.ShapeD...  47.6 us
    all_to_all x1, blocking collectives, local(): lax.all_to_all(snapshots, 'tile', split_axis=1, concat_axis=0, tiled=True)  20.8 us
    dot_general x1, matrix products, local(): lax.dot_general(c, old_basis, (((1,), (1,)), ((), ())), precision=HIGH, p...  6 us
  transfers between devices with their start and end apart: 1, of which 1 were waited for; matrix products, arithmetic and copies ran while one was open for 0% of the time, Pallas kernels for 0%

profile of v1, /device:TPU:1, one launch (start us, length us, event | category | flops | bytes accessed | tf_op | source)
XLA Modules:
  0.0 297.3 jit_solution(8071598506179631754)
XLA Ops:
  6.5 0.0 all-reduce.2.cloned.1.call-start
  6.5 20.8 %all_to_all.19 = f32[2,32,1920]{2,0,1:T(2,128)S(1)} all-to-all(f32[2,32,1920]{2,0,1:T(2,128)} %bitcast.10), channel_id=1, replica_groups=mesh['tile'=32,'slab'=4] {'tile'}, dimensions={1} | all-to-all | bytes 983040 | tf_op jit(solution)/shard_map/all_to_all | solution.py:172
  27.3 0.3 all_to_all.17.x_ref
  27.7 5.3 %fusion = f32[64,512]{1,0:T(8,128)} fusion(f32[64,1920]{1,0:T(8,128)S(1)} %all_to_all.17.x_ref, f32[1920,512]{1,0:T(8,128)} %u_ref.1), kind=kOutput, calls=%fused_computation.3 | convolution fusion | flops 754974720 | bytes 4554752 | tf_op jit(solution)/shard_map/dot_general | solution.py:175
  32.9 0.0 copy-start.1
  32.9 0.0 all-reduce.2.cloned.1.call-update
  33.0 137.6 %all-reduce.2.cloned.1.call-done = f32[64,512]{1,0:T(8,128)} async-done(((f32[64,512]{1,0:T(8,128)}), f32[64,512]{1,0:T(8,128)}) %all-reduce.2.cloned.1.call-update) | async-done | bytes 131088 | tf_op jit(solution)/shard_map/psum | solution.py:176
  170.6 0.0 copy-start.2
  170.6 6.0 %convolution_subtract_fusion = f32[64,1920]{1,0:T(8,128)S(1)} fusion(f32[64,1920]{1,0:T(8,128)S(1)} %all_to_all.17.x_ref, f32[1920,512]{1,0:T(8,128)} %u_ref.1, f32[64,512]{1,0:T(8,128)} %all-reduce.2.cloned.1.call-done), kind=kOutput, calls=%fused_computation | convolution fusion | flops 755130368 | bytes 5046272 | tf_op jit(solution)/shard_map/dot_general | solution.py:177
  176.6 0.6 fusion.1
  177.2 63.4 %psum.15 = f32[64,64]{1,0:T(8,128)S(1)} all-reduce(f32[64,64]{1,0:T(8,128)S(1)} %fusion.1), channel_id=1, replica_groups=mesh['tile'=32,'slab'=4] {'tile','slab'}, use_global_device_ids=true, to_apply=%region_1.0 | all-reduce | flops 4096 | bytes 32768 | tf_op jit(solution)/shard_map/psum | solution.py:179
  240.6 0.0 copy-done.2
  240.7 0.0 copy-done.1
  240.7 0.0 copy-start
  240.7 2.1 copy-done
  242.8 47.6 %shard_map.37 = bf16[1920,512]{1,0:T(8,128)(2,1)} custom-call(f32[64,512]{1,0:T(8,128)S(1)} %broadcast_multiply_fusion.c_ref, f32[64,64]{1,0:T(8,128)S(1)} %broadcast_multiply_fusion.1.k_ref, f32[1,512]{1,0:T(1,128)S(1)} %bitcast.8, f32[64,1920]{1,0:T(8,128)S(1)} %all_to_all.17.x_ref, f32[1920,512]{1,0:T(8,128)S(1)} %copy-done), custom_call_target="tpu_custom_call" | custom-call | flops 3019898880 | bytes 5898240 | tf_op jit(solution)/shard_map/pallas_call | solution.py:149
  (2 shorter events, 0.0 us)
Async XLA Ops:
  6.5 164.1 %all-reduce.2.cloned.1.call-start = ((), (), s32[]{:S(2)}) async-start(), calls=%async_computation.1 | async-start | bytes 262144 | tf_op jit(solution)/shard_map/psum | solution.py:176
  32.9 207.7 %copy-start.1 = (f32[512]{0:T(512)S(1)}, f32[512]{0:T(512)}, u32[]{:S(2)}) copy-start(f32[512]{0:T(512)} %param.5) | copy-start | bytes 6148
  170.6 70.0 %copy-start.2 = (f32[64,512]{1,0:T(8,128)S(1)}, f32[64,512]{1,0:T(8,128)}, u32[]{:S(2)}) copy-start(f32[64,512]{1,0:T(8,128)} %all-reduce.2.cloned.1.call-done) | copy-start | bytes 393220
  240.7 2.1 copy-start
Sparse Core Ops, SparseCore 0:
  33.1 137.4 all-reduce.1

commit v2 on v1

--- a/solution.py
+++ b/solution.py
@@ -124,6 +124,201 @@
     return w - dot1(w.astype(BF16), half), v - dot1(v.astype(BF16), half)
 
 
+def all_reduce(part, held, shared, total, sends, arrivals, scale):
+    me, slab = lax.axis_index("tile"), lax.axis_index("slab")
+    core, spot = lax.rem(me, 2), me // 2
+    twin = slab * 2 + core
+    spots, twins = part.shape[0], shared.shape[0]
+    waits = []
+
+    def put(src, dst, base, step, slot, device):
+        copy = pltpu.make_async_remote_copy(
+            src_ref=src,
+            dst_ref=dst,
+            send_sem=sends.at[base + step],
+            recv_sem=arrivals.at[base + slot],
+            device_id=device,
+            device_id_type=pl.DeviceIdType.MESH,
+        )
+        copy.start()
+        waits.append(copy)
+
+    def take(buf, base, slot):
+        pltpu.make_async_remote_copy(
+            src_ref=buf.at[slot],
+            dst_ref=buf.at[slot],
+            send_sem=sends.at[base],
+            recv_sem=arrivals.at[base + slot],
+            device_id=(me, slab),
+            device_id_type=pl.DeviceIdType.MESH,
+        ).wait_recv()
+
+    for d in range(1, spots):
+        peer = lax.rem(spot + d, spots)
+        put(part.at[peer], held.at[spot], 0, d, spot, (2 * peer + core, slab))
+    held[spot] = part[spot]
+    for d in range(1, spots):
+        take(held, 0, lax.rem(spot + d, spots))
+    shared[twin] = jnp.sum(held[...], axis=0)
+    for d in range(1, twins):
+        peer = lax.rem(twin + d, twins)
+        put(shared.at[twin], shared.at[twin], spots, d, twin, (2 * spot + lax.rem(peer, 2), peer // 2))
+    for d in range(1, twins):
+        take(shared, spots, lax.rem(twin + d, twins))
+    total[spot] = jnp.sum(shared[...], axis=0) * scale
+    for d in range(1, spots):
+        peer = lax.rem(spot + d, spots)
+        put(total.at[spot], total.at[spot], spots + twins, d, spot, (2 * peer + core, slab))
+    for d in range(1, spots):
+        take(total, spots + twins, lax.rem(spot + d, spots))
+    return waits
+
+
+def gather_kernel(
+    scale, snap_ref, u_ref, c_ref, k_ref, x_ref,
+    u_vm, uh_ref, ul_ref, got, cpart, cheld, cshared, ctotal, kpart, kheld, kshared, ktotal,
+    u_sem, own_sem, x_send, x_recv, c_send, c_recv, k_send, k_recv,
+):
+    me, slab = lax.axis_index("tile"), lax.axis_index("slab")
+    tiles = got.shape[0]
+    cells = u_vm.shape[0]
+    load = pltpu.make_async_copy(u_ref, u_vm, u_sem)
+    load.start()
+    core, spot = lax.rem(me, 2), me // 2
+    twin = slab * 2 + core
+    twins = cshared.shape[0]
+    barrier = pltpu.get_barrier_semaphore()
+    for d in range(1, tiles):
+        pl.semaphore_signal(
+            barrier, inc=1, device_id=(lax.rem(me + d, tiles), slab), device_id_type=pl.DeviceIdType.MESH
+        )
+    for d in range(1, twins):
+        peer = lax.rem(twin + d, twins)
+        pl.semaphore_signal(
+            barrier, inc=1, device_id=(2 * spot + lax.rem(peer, 2), peer // 2), device_id_type=pl.DeviceIdType.MESH
+        )
+    pl.semaphore_wait(barrier, tiles + twins - 2)
+
+    def cut(tile):
+        return snap_ref.at[:, pl.ds(pl.multiple_of(tile * cells, 128), cells)]
+
+    waits = []
+    for d in range(1, tiles):
+        peer = lax.rem(me + d, tiles)
+        copy = pltpu.make_async_remote_copy(
+            src_ref=cut(peer),
+            dst_ref=got.at[me],
+            send_sem=x_send.at[d],
+            recv_sem=x_recv.at[me],
+            device_id=(peer, slab),
+            device_id_type=pl.DeviceIdType.MESH,
+        )
+        copy.start()
+        waits.append(copy)
+    own = pltpu.make_async_copy(cut(me), got.at[me], own_sem)
+    own.start()
+    load.wait()
+    step = 192
+
+    @pl.loop(0, cells // step)
+    def _(i):
+        at = pl.ds(pl.multiple_of(i * step, step), step)
+        hi, lo = split(u_vm[at, :])
+        uh_ref[at, :] = hi
+        ul_ref[at, :] = lo
+
+    own.wait()
+    for d in range(1, tiles):
+        slot = lax.rem(me + d, tiles)
+        pltpu.make_async_remote_copy(
+            src_ref=got.at[slot],
+            dst_ref=got.at[slot],
+            send_sem=x_send.at[0],
+            recv_sem=x_recv.at[slot],
+            device_id=(me, slab),
+            device_id_type=pl.DeviceIdType.MESH,
+        ).wait_recv()
+    x = jnp.concatenate([got[:, 0, :], got[:, 1, :]], axis=0)
+    x_ref[...] = x
+    snaps = x.shape[0]
+    xh, xl = split(x)
+    both = dot1(jnp.concatenate([xh, xl], axis=0), uh_ref[...])
+    part = both[:snaps] + both[snaps:] + dot1(xh, ul_ref[...])
+    rows, cols = cpart.shape[1:]
+    across = part.shape[1] // cols
+    for i in range(cpart.shape[0]):
+        r, l = divmod(i, across)
+        cpart[i] = part[r * rows : (r + 1) * rows, l * cols : (l + 1) * cols]
+    waits += all_reduce(cpart, cheld, cshared, ctotal, c_send, c_recv, scale)
+    for i in range(cpart.shape[0]):
+        r, l = divmod(i, across)
+        c_ref[r * rows : (r + 1) * rows, l * cols : (l + 1) * cols] = ctotal[i]
+    ch, cl = split(c_ref[...])
+    both = dot1(jnp.concatenate([ch, cl], axis=0), uh_ref[...], 1, 1)
+    resid = x_ref[...] - (both[:snaps] + both[snaps:] + dot1(ch, ul_ref[...], 1, 1))
+    square = dot3(resid, resid, 1, 1)
+    half = snaps // 2
+    packed = jnp.concatenate([square[:half], square[half:]], axis=1)
+    krows = kpart.shape[1]
+    for i in range(kpart.shape[0]):
+        kpart[i] = packed[i * krows : (i + 1) * krows]
+    waits += all_reduce(kpart, kheld, kshared, ktotal, k_send, k_recv, scale)
+    packed = jnp.concatenate([ktotal[i] for i in range(kpart.shape[0])], axis=0)
+    k_ref[:half, :] = packed[:, :snaps]
+    k_ref[half:, :] = packed[:, snaps:]
+    for copy in waits:
+        copy.wait_send()
+
+
+def gather(snapshots, u, tiles, slabs, scale):
+    cells, modes = u.shape
+    each = snapshots.shape[0]
+    snaps = each * tiles
+    spots, twins = tiles // 2, 2 * slabs
+    crows, ccols = 8, snaps * modes // (8 * spots)
+    krows = snaps // 2 // spots
+    vmem = pl.BlockSpec(memory_space=pltpu.VMEM)
+    dma = lambda n: pltpu.SemaphoreType.DMA((n,))
+    block = lambda n, *shape: pltpu.VMEM((n, *shape), F32)
+    steps = 2 * spots + twins
+    return pl.pallas_call(
+        functools.partial(gather_kernel, scale),
+        out_shape=(
+            jax.ShapeDtypeStruct((snaps, modes), F32),
+            jax.ShapeDtypeStruct((snaps, snaps), F32),
+            jax.ShapeDtypeStruct((snaps, cells), F32),
+        ),
+        in_specs=[pl.BlockSpec(memory_space=pl.ANY)] * 2,
+        out_specs=(vmem, vmem, vmem),
+        scratch_shapes=[
+            pltpu.VMEM((cells, modes), F32),
+            pltpu.VMEM((cells, modes), BF16),
+            pltpu.VMEM((cells, modes), BF16),
+            block(tiles, each, cells),
+            block(spots, crows, ccols),
+            block(spots, crows, ccols),
+            block(twins, crows, ccols),
+            block(spots, crows, ccols),
+            block(spots, krows, 2 * snaps),
+            block(spots, krows, 2 * snaps),
+            block(twins, krows, 2 * snaps),
+            block(spots, krows, 2 * snaps),
+            pltpu.SemaphoreType.DMA,
+            pltpu.SemaphoreType.DMA,
+            dma(tiles),
+            dma(tiles),
+            dma(steps),
+            dma(steps),
+            dma(steps),
+            dma(steps),
+        ],
+        compiler_params=pltpu.CompilerParams(
+            collective_id=0, has_side_effects=True, vmem_limit_bytes=40 * 2**20
+        ),
+        cost_estimate=pl.CostEstimate(flops=2 * 6 * snaps * cells * modes, bytes_accessed=4 * cells * modes, transcendentals=0),
+    )(snapshots, u)
+
+
 def update_kernel(c_ref, k_ref, s_ref, x_ref, u_ref, o_ref, wh_ref, wl_ref, vs_ref):
     @pl.when(pl.program_id(0) == 0)
     def _():
@@ -169,14 +364,9 @@
 
 
 def local(snapshots, old_basis, sing_values):
-    x = lax.all_to_all(snapshots, "tile", split_axis=1, concat_axis=0, tiled=True)
-    cells = old_basis.shape[0] * lax.axis_size("tile") * lax.axis_size("slab")
-    weight = 1.0 / cells
-    c = jnp.dot(x, old_basis, precision=HIGH, preferred_element_type=F32)
-    c = lax.psum(c, ("tile", "slab")) * weight
-    resid = x - lax.dot_general(c, old_basis, (((1,), (1,)), ((), ())), precision=HIGH, preferred_element_type=F32)
-    k_res = lax.dot_general(resid, resid, (((1,), (1,)), ((), ())), precision=HIGH, preferred_element_type=F32)
-    k_res = lax.psum(k_res, ("tile", "slab")) * weight
+    tiles, slabs = lax.axis_size("tile"), lax.axis_size("slab")
+    cells = old_basis.shape[0] * tiles * slabs
+    c, k_res, x = gather(snapshots, old_basis, tiles, slabs, 1.0 / cells)
     return update(c, k_res, sing_values[None], x, old_basis)
 
 

time: 298 us -> 98.5 us (0.33)
  waiting for transfers between devices: 138 us -> 0 us
  blocking collectives: 84.2 us -> 0 us
  Pallas kernels: 47.6 us -> 95.1 us
  between operations: 13.4 us -> 0.03 us
  matrix products: 11.8 us -> 0 us
    psum x1 -> x0, waiting for transfers between devices: 138 us -> none  [local(): c = lax.psum(c, ('tile', 'slab')) * weight]
    psum x1 -> x0, blocking collectives: 63.4 us -> none  [local(): k_res = lax.psum(k_res, ('tile', 'slab')) * weight]
    pallas_call x0 -> x1, Pallas kernels: none -> 47.4 us  [gather(): pl.pallas_call(functools.partial(gather_kernel, scale), out_shape=(jax.Sh...]
    all_to_all x1 -> x0, blocking collectives: 20.8 us -> none  [local(): lax.all_to_all(snapshots, 'tile', split_axis=1, concat_axis=0, tiled=True)]
    dot_general x3 -> x0, matrix products: 11.8 us -> none  [the longest x1 6 us: local(): lax.dot_general(c, old_basis, (((1,), (1,)), ((), ())), precision=HIGH, p...]
  transfers between devices with their start and end apart: 1 -> 0, of which waited for: 1 -> 0; matrix products, arithmetic and copies ran while one was open for 0% -> 0% of each run, Pallas kernels for 0% -> 0%
where the time goes in v2:
time: 98.5 us; the launch traced here: 98.3 us
  Pallas kernels  95.1 us (97%)
  local copies, waits for them, and re-layouts  3.15 us (3%)
    pallas_call x1, Pallas kernels, update(): pl.pallas_call(update_kernel, grid=(cells // rows,), out_shape=jax.ShapeD...  47.7 us
    pallas_call x1, Pallas kernels, gather(): pl.pallas_call(functools.partial(gather_kernel, scale), out_shape=(jax.Sh...  47.4 us
    unnamed x8, local copies, waits for them, and re-layouts  3.15 us

profile of v2, /device:TPU:1, one launch (start us, length us, event | category | flops | bytes accessed | tf_op | source)
XLA Modules:
  0.0 98.3 jit_solution(14178062739367983815)
XLA Ops:
  0.0 0.0 copy-start
  0.0 2.1 %copy-done = f32[1920,512]{1,0:T(8,128)S(1)} copy-done((f32[1920,512]{1,0:T(8,128)S(1)}, f32[1920,512]{1,0:T(8,128)}, u32[]{:S(2)}) %copy-start) | copy-done | bytes 3932184
  2.1 0.0 copy-start.2
  2.1 1.0 %copy-done.2 = f32[2,61440]{1,0:T(2,128)S(1)} copy-done((f32[2,61440]{1,0:T(2,128)S(1)}, f32[2,61440]{1,0:T(2,128)}, u32[]{:S(2)}) %copy-start.2) | copy-done | bytes 491544
  3.1 0.0 copy-start.1
  3.1 0.0 copy-start.3
  3.1 47.4 %shard_map.37 = (f32[64,512]{1,0:T(8,128)S(1)}, f32[64,64]{1,0:T(8,128)S(1)}, f32[64,1920]{1,0:T(8,128)S(1)}) custom-call(f32[2,61440]{1,0:T(2,128)S(1)} %copy-done.2, f32[1920,512]{1,0:T(8,128)S(1)} %copy-done), custom_call_target="tpu_custom_call" | custom-call | flops 754974720 | bytes 3932160 | tf_op jit(solution)/shard_map/pallas_call | solution.py:284
  50.6 0.0 copy-done.1
  50.6 0.0 copy-done.3
  50.6 47.7 %shard_map.38 = bf16[1920,512]{1,0:T(8,128)(2,1)} custom-call(f32[64,512]{1,0:T(8,128)S(1)} %get-tuple-element.8.c_ref, f32[64,64]{1,0:T(8,128)S(1)} %get-tuple-element.9.k_ref, f32[1,512]{1,0:T(1,128)S(1)} %bitcast.1, f32[64,1920]{1,0:T(8,128)S(1)} %get-tuple-element.10.x_ref, f32[1920,512]{1,0:T(8,128)S(1)} %copy-done.1), custom_call_target="tpu_custom_call" | custom-call | flops 3019898880 | bytes 5898240 | tf_op jit(solution)/shard_map/pallas_call | solution.py:344
Async XLA Ops:
  0.0 2.1 %copy-start = (f32[1920,512]{1,0:T(8,128)S(1)}, f32[1920,512]{1,0:T(8,128)}, u32[]{:S(2)}) copy-start(f32[1920,512]{1,0:T(8,128)} %u_ref.3) | copy-start | bytes 11796484
  2.1 1.0 %copy-start.2 = (f32[2,61440]{1,0:T(2,128)S(1)}, f32[2,61440]{1,0:T(2,128)}, u32[]{:S(2)}) copy-start(f32[2,61440]{1,0:T(2,128)} %snap_ref.1) | copy-start | bytes 1474564
  3.1 47.4 %copy-start.1 = (f32[1920,512]{1,0:T(8,128)S(1)}, f32[1920,512]{1,0:T(8,128)}, u32[]{:S(2)}) copy-start(f32[1920,512]{1,0:T(8,128)} %u_ref.3) | copy-start | bytes 11796484
  3.1 47.4 %copy-start.3 = (f32[512]{0:T(512)S(1)}, f32[512]{0:T(512)}, u32[]{:S(2)}) copy-start(f32[512]{0:T(512)} %param.5) | copy-start | bytes 6148

commit v3 on v2

--- a/solution.py
+++ b/solution.py
@@ -30,32 +30,70 @@
     return dot1(ah, bh, ca, cb) + (dot1(ah, bl, ca, cb) + dot1(al, bh, ca, cb))
 
 
+def inverse_pairs(pairs, wide=4):
+    n = pairs[0].shape[0]
+    full = (8, 2 * n)
+    sub = lax.broadcasted_iota(jnp.int32, full, 0)
+    lane = lax.broadcasted_iota(jnp.int32, full, 1)
+    own, base = lane % n, (lane // n) * n
+    work = [[a[8 * r : 8 * r + 8] for r in range(n // 8)] for a in pairs]
+    done = [[None] * n for _ in pairs]
+
+    def spread(v, at):
+        return jnp.take_along_axis(v, base + at, axis=1)
+
+    for j in range(0, n, wide):
+        r, s = divmod(j, 8)
+        first = r if s + wide < 8 else r + 1
+        inside = (own >= j) & (own < j + wide)
+        for m, rows in enumerate(work):
+            row = [jnp.broadcast_to(rows[r][s + i : s + i + 1, :], full) for i in range(wide)]
+            e = {(i, l): spread(row[i], j + l) for i in range(wide) for l in range(i, wide)}
+            col = {(q, i): spread(rows[q], j + i) for q in range(first, n // 8) for i in range(wide)}
+            if first == r:
+                for i in range(wide):
+                    col[r, i] = jnp.where(sub >= s + wide, col[r, i], 0.0)
+            row = [jnp.where(inside, jnp.where(own == j + i, 1.0, 0.0), row[i]) for i in range(wide)]
+            part, f = [], {}
+            for i in range(wide):
+                inv = 1.0 / e[i, i]
+                part.append(row[i] * inv)
+                done[m][j + i] = row[i] * lax.rsqrt(e[i, i])
+                for l in range(i + 1, wide):
+                    f[i, l] = e[i, l] * inv
+                    row[l] = row[l] - f[i, l] * row[i]
+                    for p in range(l, wide):
+                        e[l, p] = e[l, p] - f[i, l] * e[i, p]
+            for i in reversed(range(wide - 1)):
+                for l in reversed(range(i + 1, wide)):
+                    part[i] = part[i] - f[i, l] * part[l]
+            for q in range(first, n // 8):
+                fall = col[q, 0] * part[0]
+                for i in range(1, wide):
+                    fall = fall + col[q, i] * part[i]
+                keep = inside & (sub >= s + wide) if q == r else inside
+                rows[q] = jnp.where(keep, 0.0, rows[q]) - fall
+    outs = []
+    for m in range(len(pairs)):
+        pieces = []
+        for r in range(n // 8):
+            piece = done[m][8 * r]
+            for s in range(1, 8):
+                piece = jnp.where(sub == s, done[m][8 * r + s], piece)
+            pieces.append(jnp.where(own <= sub + 8 * r, piece, 0.0))
+        outs.append(jnp.concatenate(pieces, axis=0))
+    return outs
+
+
 def inverse_factors(mats):
     n = mats[0].shape[0]
-    eye = (lax.broadcasted_iota(jnp.int32, (n, n), 0) == lax.broadcasted_iota(jnp.int32, (n, n), 1)).astype(F32)
-    sub = lax.broadcasted_iota(jnp.int32, (8, 2 * n), 0)
-    work = []
-    for a in mats:
-        both = jnp.concatenate([eye, a], axis=1)
-        work.append([both[8 * r : 8 * r + 8] for r in range(n // 8)])
-    scale = [[None] * (n // 8) for _ in mats]
-    for j in range(n):
-        r, s = divmod(j, 8)
-        for m, rows in enumerate(work):
-            row = jnp.broadcast_to(rows[r][s : s + 1, :], (8, 2 * n))
-            pivot = jnp.broadcast_to(row[:, n + j : n + j + 1], (8, 2 * n))
-            part = row * (1.0 / pivot)
-            root = lax.rsqrt(pivot)
-            scale[m][r] = root if s == 0 else jnp.where(sub == s, root, scale[m][r])
-            for q in range(r, n // 8):
-                col = jnp.broadcast_to(rows[q][:, n + j : n + j + 1], (8, 2 * n))
-                if q == r:
-                    col = jnp.where(sub > s, col, 0.0)
-                rows[q] = rows[q] - col * part
-    return [
-        jnp.concatenate([rows[r] * scale[m][r] for r in range(n // 8)], axis=0)[:, :n]
-        for m, rows in enumerate(work)
-    ]
+    odd = len(mats) % 2
+    mats = mats + mats[:1] * odd
+    pairs = [jnp.concatenate(mats[i : i + 2], axis=1) for i in range(0, len(mats), 2)]
+    outs = []
+    for p in inverse_pairs(pairs):
+        outs += [p[:, :n], p[:, n:]]
+    return outs[: len(outs) - odd]
 
 
 def weights_of(c, k_res, sing, second=True):
@@ -124,59 +162,83 @@
     return w - dot1(w.astype(BF16), half), v - dot1(v.astype(BF16), half)
 
 
-def all_reduce(part, held, shared, total, sends, arrivals, scale):
-    me, slab = lax.axis_index("tile"), lax.axis_index("slab")
-    core, spot = lax.rem(me, 2), me // 2
-    twin = slab * 2 + core
-    spots, twins = part.shape[0], shared.shape[0]
-    waits = []
-
-    def put(src, dst, base, step, slot, device):
+def route(sends, arrivals):
+    started = []
+
+    def put(src, dst, step, slot, device):
         copy = pltpu.make_async_remote_copy(
             src_ref=src,
             dst_ref=dst,
-            send_sem=sends.at[base + step],
-            recv_sem=arrivals.at[base + slot],
+            send_sem=sends.at[step],
+            recv_sem=arrivals.at[slot],
             device_id=device,
             device_id_type=pl.DeviceIdType.MESH,
         )
         copy.start()
-        waits.append(copy)
-
-    def take(buf, base, slot):
+        started.append(copy)
+
+    def take(buf, at, slot):
         pltpu.make_async_remote_copy(
-            src_ref=buf.at[slot],
-            dst_ref=buf.at[slot],
-            send_sem=sends.at[base],
-            recv_sem=arrivals.at[base + slot],
-            device_id=(me, slab),
+            src_ref=buf.at[at],
+            dst_ref=buf.at[at],
+            send_sem=sends.at[0],
+            recv_sem=arrivals.at[slot],
+            device_id=(lax.axis_index("tile"), lax.axis_index("slab")),
             device_id_type=pl.DeviceIdType.MESH,
         ).wait_recv()
 
+    return put, take, started
+
+
+def place():
+    me, slab = lax.axis_index("tile"), lax.axis_index("slab")
+    core, spot = lax.rem(me, 2), me // 2
+    return me, slab, core, spot, slab * 2 + core
+
+
+def share(buf, base, far, put, take):
+    me, slab, core, spot, twin = place()
+    n, mine = buf.shape[0], spot if far else twin
+    for d in range(1, n):
+        peer = lax.rem(mine + d, n)
+        device = (2 * peer + core, slab) if far else (2 * spot + lax.rem(peer, 2), peer // 2)
+        put(buf.at[mine], buf.at[mine], base + d, base + mine, device)
+    for d in range(1, n):
+        slot = lax.rem(mine + d, n)
+        take(buf, slot, base + slot)
+
+
+def sum_by_owner(part, held, shared, total, sends, arrivals, scale):
+    me, slab, core, spot, twin = place()
+    spots, twins = part.shape[0], shared.shape[0]
+    put, take, started = route(sends, arrivals)
     for d in range(1, spots):
         peer = lax.rem(spot + d, spots)
-        put(part.at[peer], held.at[spot], 0, d, spot, (2 * peer + core, slab))
+        put(part.at[peer], held.at[spot], d, spot, (2 * peer + core, slab))
     held[spot] = part[spot]
     for d in range(1, spots):
-        take(held, 0, lax.rem(spot + d, spots))
+        slot = lax.rem(spot + d, spots)
+        take(held, slot, slot)
     shared[twin] = jnp.sum(held[...], axis=0)
-    for d in range(1, twins):
-        peer = lax.rem(twin + d, twins)
-        put(shared.at[twin], shared.at[twin], spots, d, twin, (2 * spot + lax.rem(peer, 2), peer // 2))
-    for d in range(1, twins):
-        take(shared, spots, lax.rem(twin + d, twins))
+    share(shared, spots, False, put, take)
     total[spot] = jnp.sum(shared[...], axis=0) * scale
-    for d in range(1, spots):
-        peer = lax.rem(spot + d, spots)
-        put(total.at[spot], total.at[spot], spots + twins, d, spot, (2 * peer + core, slab))
-    for d in range(1, spots):
-        take(total, spots + twins, lax.rem(spot + d, spots))
-    return waits
+    share(total, spots + twins, True, put, take)
+    return started
+
+
+def sum_whole(part, far, near, sends, arrivals, scale):
+    me, slab, core, spot, twin = place()
+    put, take, started = route(sends, arrivals)
+    near[twin] = part
+    share(near, 0, False, put, take)
+    far[spot] = jnp.sum(near[...], axis=0)
+    share(far, near.shape[0], True, put, take)
+    return jnp.sum(far[...], axis=0) * scale, started
 
 
 def gather_kernel(
     scale, snap_ref, u_ref, c_ref, k_ref, x_ref,
-    u_vm, uh_ref, ul_ref, got, cpart, cheld, cshared, ctotal, kpart, kheld, kshared, ktotal,
+    u_vm, uh_ref, ul_ref, got, cpart, cheld, cshared, ctotal, kfar, knear,
     u_sem, own_sem, x_send, x_recv, c_send, c_recv, k_send, k_recv,
 ):
     me, slab = lax.axis_index("tile"), lax.axis_index("slab")
@@ -249,7 +311,7 @@
     for i in range(cpart.shape[0]):
         r, l = divmod(i, across)
         cpart[i] = part[r * rows : (r + 1) * rows, l * cols : (l + 1) * cols]
-    waits += all_reduce(cpart, cheld, cshared, ctotal, c_send, c_recv, scale)
+    waits += sum_by_owner(cpart, cheld, cshared, ctotal, c_send, c_recv, scale)
     for i in range(cpart.shape[0]):
         r, l = divmod(i, across)
         c_ref[r * rows : (r + 1) * rows, l * cols : (l + 1) * cols] = ctotal[i]
@@ -259,11 +321,8 @@
     square = dot3(resid, resid, 1, 1)
     half = snaps // 2
     packed = jnp.concatenate([square[:half], square[half:]], axis=1)
-    krows = kpart.shape[1]
-    for i in range(kpart.shape[0]):
-        kpart[i] = packed[i * krows : (i + 1) * krows]
-    waits += all_reduce(kpart, kheld, kshared, ktotal, k_send, k_recv, scale)
-    packed = jnp.concatenate([ktotal[i] for i in range(kpart.shape[0])], axis=0)
+    packed, more = sum_whole(packed, kfar, knear, k_send, k_recv, scale)
+    waits += more
     k_ref[:half, :] = packed[:, :snaps]
     k_ref[half:, :] = packed[:, snaps:]
     for copy in waits:
@@ -276,7 +335,6 @@
     snaps = each * tiles
     spots, twins = tiles // 2, 2 * slabs
     crows, ccols = 8, snaps * modes // (8 * spots)
-    krows = snaps // 2 // spots
     vmem = pl.BlockSpec(memory_space=pltpu.VMEM)
     dma = lambda n: pltpu.SemaphoreType.DMA((n,))
     block = lambda n, *shape: pltpu.VMEM((n, *shape), F32)
@@ -299,21 +357,19 @@
             block(spots, crows, ccols),
             block(twins, crows, ccols),
             block(spots, crows, ccols),
-            block(spots, krows, 2 * snaps),
-            block(spots, krows, 2 * snaps),
-            block(twins, krows, 2 * snaps),
-            block(spots, krows, 2 * snaps),
+            block(spots, snaps // 2, 2 * snaps),
+            block(twins, snaps // 2, 2 * snaps),
             pltpu.SemaphoreType.DMA,
             pltpu.SemaphoreType.DMA,
             dma(tiles),
             dma(tiles),
             dma(steps),
             dma(steps),
-            dma(steps),
-            dma(steps),
+            dma(spots + twins),
+            dma(spots + twins),
         ],
         compiler_params=pltpu.CompilerParams(
-            collective_id=0, has_side_effects=True, vmem_limit_bytes=40 * 2**20
+            collective_id=0, has_side_effects=True, vmem_limit_bytes=60 * 2**20
         ),
         cost_estimate=pl.CostEstimate(flops=2 * 6 * snaps * cells * modes, bytes_accessed=4 * cells * modes, transcendentals=0),
     )(snapshots, u)
@@ -358,7 +414,7 @@
             pltpu.VMEM((modes, modes), BF16),
             pltpu.VMEM((3 * snaps, modes), BF16),
         ],
-        compiler_params=pltpu.CompilerParams(vmem_limit_bytes=48 * 2**20),
+        compiler_params=pltpu.CompilerParams(vmem_limit_bytes=60 * 2**20),
         cost_estimate=pl.CostEstimate(flops=2 * 3 * cells * modes * modes, bytes_accessed=6 * cells * modes, transcendentals=0),
     )(c, k_res, sing, x, u)
 

time: 98.5 us -> 80.2 us (0.81)
  Pallas kernels: 95.1 us -> 79.9 us
  local copies, waits for them, and re-layouts: 3.15 us -> 0 us
    pallas_call x1, Pallas kernels: 47.7 us -> 34.4 us  [update(): pl.pallas_call(update_kernel, grid=(cells // rows,), out_shape=jax.ShapeD...]
    unnamed x8 -> x0, local copies, waits for them, and re-layouts: 3.15 us -> none
    pallas_call x1, Pallas kernels: 47.4 us -> 45.5 us  [gather(): pl.pallas_call(functools.partial(gather_kernel, scale), out_shape=(jax.Sh...]
where the time goes in v3:
time: 80.2 us; the launch traced here: 79.9 us
  Pallas kernels  79.9 us (100%)
    pallas_call x1, Pallas kernels, gather(): pl.pallas_call(functools.partial(gather_kernel, scale), out_shape=(jax.Sh...  45.5 us
    pallas_call x1, Pallas kernels, update(): pl.pallas_call(update_kernel, grid=(cells // rows,), out_shape=jax.ShapeD...  34.4 us

profile of v3, /device:TPU:1, one launch (start us, length us, event | category | flops | bytes accessed | tf_op | source)
XLA Modules:
  0.0 79.9 jit_solution(11526142919772388226)
XLA Ops:
  0.0 45.5 %shard_map.37 = (f32[64,512]{1,0:T(8,128)}, f32[64,64]{1,0:T(8,128)}, f32[64,1920]{1,0:T(8,128)}) custom-call(f32[2,61440]{1,0:T(2,128)} %snap_ref.1, f32[1920,512]{1,0:T(8,128)} %u_ref.3), custom_call_target="tpu_custom_call" | custom-call | flops 754974720 | bytes 3932160 | tf_op jit(solution)/shard_map/pallas_call | solution.py:342
  45.5 34.4 %shard_map.38 = bf16[1920,512]{1,0:T(8,128)(2,1)} custom-call(f32[64,512]{1,0:T(8,128)} %get-tuple-element.8.c_ref, f32[64,64]{1,0:T(8,128)} %get-tuple-element.9.k_ref, f32[1,512]{1,0:T(1,128)} %bitcast.1, f32[64,1920]{1,0:T(8,128)} %get-tuple-element.10.x_ref, f32[1920,512]{1,0:T(8,128)} %u_ref.3), custom_call_target="tpu_custom_call" | custom-call | flops 3019898880 | bytes 5898240 | tf_op jit(solution)/shard_map/pallas_call | solution.py:400
